TPU v7x, 32 devices: a whole 2x2x4 slice. The times are simulated.
32 devices in a mesh: expert: 8 (over y, x, core), dp: 4 (over z).
Axes of the slice: x: 2, y: 2, z: 4, core: 2. Of those that a mesh axis runs over, the one named last changes fastest.
Arguments:
- tokens: bfloat16 [4096, 1024], P(('expert', 'dp')), may hold values from -6 to 6
- expert_ids: int32 [4096, 2], P(('expert', 'dp')), may hold values from 0 to 7, as said below
- slot_index: int32 [4096, 2], P(('expert', 'dp')), may hold values from 0 to 39, as said below
- keep_mask: int32 [4096, 2], P(('expert', 'dp')), may hold values from 0 to 1, as said below
- route_weight: float32 [4096, 2], P(('expert', 'dp')), may hold values from 0.2 to 1
- cotangent: bfloat16 [4096, 1024], P(('expert', 'dp')), may hold values from -6 to 6
- w_gate: bfloat16 [8, 1024, 768], P('expert'), may hold values from -0.1875 to 0.1875
- w_up: bfloat16 [8, 1024, 768], P('expert'), may hold values from -0.1875 to 0.1875
- w_down: bfloat16 [8, 768, 1024], P('expert'), may hold values from -0.21875 to 0.21875
Outputs:
- layer_output: bfloat16 [4096, 1024], P(('expert', 'dp'))
- route_grad: float32 [4096, 2], P(('expert', 'dp'))
- input_grad: bfloat16 [4096, 1024], P(('expert', 'dp'))
- gate_grad: float32 [8, 1024, 768], P('expert', None, 'dp')
- up_grad: float32 [8, 1024, 768], P('expert', None, 'dp')
- down_grad: float32 [8, 768, 1024], P('expert', 'dp')
Inputs may be any that keep to these rules, and one draw needn't show every extreme that they name: `expert_ids`: the two experts of a token differ. In every index of dp, one expert gets 40 or more routes from every device of that index, and it differs from index to index as drawn. `slot_index`: A route's slot is its rank among the routes of its device's block of 128 tokens to the same expert, counted token by token with the first route before the second; routes of rank 40 or more have slot 39. `keep_mask`: A route is kept exactly when its rank is under 40, so kept routes of one block to one expert have distinct slots, and in every block some expert has all 40 slots kept.
All inputs are finite; a program needn't handle non-finite values.
Results may differ from a plain program's by a relative error of at most 0.0085.
Values may be sent and summed in bfloat16 or wider, within the bound.
A program may use at most 64 MiB of HBM per device.

v0:
```python
import jax
import jax.numpy as jnp
from jax import lax
from jax.sharding import PartitionSpec as P


def expert_forward(rows_in, gate_mat, up_mat, down_mat):
    gate_value = jnp.dot(rows_in, gate_mat, preferred_element_type=jnp.float32)
    up_value = jnp.dot(rows_in, up_mat, preferred_element_type=jnp.float32)
    sigmoid_gate = jax.nn.sigmoid(gate_value)
    activation = (gate_value * sigmoid_gate * up_value).astype(jnp.bfloat16)
    expert_out = jnp.dot(activation, down_mat, preferred_element_type=jnp.float32).astype(
        jnp.bfloat16
    )
    return (gate_value, up_value, sigmoid_gate, activation, expert_out)


def value_grads(rows_grad, down_mat, gate_value, up_value, sigmoid_gate):
    act_grad = lax.dot_general(
        rows_grad, down_mat, (((1,), (1,)), ((), ())), preferred_element_type=jnp.float32
    )
    up_value_grad = (act_grad * gate_value * sigmoid_gate).astype(jnp.bfloat16)
    gate_value_grad = (
        act_grad * up_value * sigmoid_gate * (1.0 + gate_value * (1.0 - sigmoid_gate))
    ).astype(jnp.bfloat16)
    return (gate_value_grad, up_value_grad)


def column_product(left, right):
    return lax.dot_general(
        left, right, (((0,), (0,)), ((), ())), preferred_element_type=jnp.float32
    )


def body(tokens, expert_ids, slot_index, keep_mask, route_weight, cotangent, w_gate, w_up, w_down):
    groups = lax.axis_size("expert")
    data_groups = lax.axis_size("dp")
    local_tokens = tokens.shape[0]
    width = tokens.shape[1]
    experts_all = groups * w_gate.shape[0]
    capacity = 5 * local_tokens // (2 * experts_all)
    gate_mat = w_gate[0]
    up_mat = w_up[0]
    down_mat = w_down[0]
    flat_index = expert_ids * capacity + slot_index
    cells = jnp.arange(experts_all * capacity, dtype=jnp.int32)
    matrix = ((flat_index[..., None] == cells) & (keep_mask[..., None] == 1)).astype(jnp.bfloat16)
    send_in = jnp.einsum("tkc,td->cd", matrix, tokens, preferred_element_type=jnp.float32)
    send_in = send_in.astype(jnp.bfloat16).reshape(experts_all, capacity, width)
    scaled = (route_weight[..., None] * cotangent[:, None, :].astype(jnp.float32)).astype(
        jnp.bfloat16
    )
    send_grad = jnp.einsum("tkc,tkd->cd", matrix, scaled, preferred_element_type=jnp.float32)
    send_grad = send_grad.astype(jnp.bfloat16).reshape(experts_all, capacity, width)
    rows_in = lax.all_to_all(send_in, "expert", split_axis=0, concat_axis=0, tiled=True)
    rows_in = rows_in.reshape(-1, width)
    gate_value, up_value, sigmoid_gate, activation, expert_out = expert_forward(
        rows_in, gate_mat, up_mat, down_mat
    )
    out_blocks = expert_out.reshape(groups, capacity, width)
    back_out = lax.all_to_all(out_blocks, "expert", split_axis=0, concat_axis=0, tiled=True)
    rows_grad = lax.all_to_all(
        send_grad, "expert", split_axis=0, concat_axis=0, tiled=True
    ).reshape(-1, width)
    part_down = column_product(activation, rows_grad)
    gate_value_grad, up_value_grad = value_grads(
        rows_grad, down_mat, gate_value, up_value, sigmoid_gate
    )
    part_gate = column_product(rows_in, gate_value_grad)
    part_up = column_product(rows_in, up_value_grad)
    gate_sum, up_sum, down_sum = (
        lax.psum_scatter(
            part_gate.astype(jnp.bfloat16), "dp", scatter_dimension=1, tiled=True
        ).astype(jnp.float32),
        lax.psum_scatter(
            part_up.astype(jnp.bfloat16), "dp", scatter_dimension=1, tiled=True
        ).astype(jnp.float32),
        lax.psum_scatter(
            part_down.astype(jnp.bfloat16), "dp", scatter_dimension=0, tiled=True
        ).astype(jnp.float32),
    )
    row_input_grad = lax.dot_general(
        gate_value_grad, gate_mat, (((1,), (1,)), ((), ())), preferred_element_type=jnp.float32
    ) + lax.dot_general(
        up_value_grad, up_mat, (((1,), (1,)), ((), ())), preferred_element_type=jnp.float32
    )
    grad_blocks = row_input_grad.astype(jnp.bfloat16).reshape(groups, capacity, width)
    back_grad = lax.all_to_all(grad_blocks, "expert", split_axis=0, concat_axis=0, tiled=True)
    back_out = back_out.reshape(-1, width)
    back_grad = back_grad.reshape(-1, width)
    picked = jnp.einsum("tkc,cd->tkd", matrix, back_out, preferred_element_type=jnp.float32)
    layer_output = jnp.sum(route_weight[..., None] * picked, axis=1).astype(jnp.bfloat16)
    route_grad = jnp.einsum(
        "td,tkd->tk", cotangent, picked.astype(jnp.bfloat16), preferred_element_type=jnp.float32
    )
    input_grad = jnp.einsum(
        "tkc,cd->td", matrix, back_grad, preferred_element_type=jnp.float32
    ).astype(jnp.bfloat16)
    scale = 1.0 / data_groups
    return (
        layer_output,
        route_grad,
        input_grad,
        (gate_sum * scale)[None],
        (up_sum * scale)[None],
        (down_sum * scale)[None],
    )


def solution(mesh):
    return jax.shard_map(
        body,
        mesh=mesh,
        in_specs=(
            P(("expert", "dp"), None),
            P(("expert", "dp"), None),
            P(("expert", "dp"), None),
            P(("expert", "dp"), None),
            P(("expert", "dp"), None),
            P(("expert", "dp"), None),
            P("expert", None, None),
            P("expert", None, None),
            P("expert", None, None),
        ),
        out_specs=(
            P(("expert", "dp"), None),
            P(("expert", "dp"), None),
            P(("expert", "dp"), None),
            P("expert", None, "dp"),
            P("expert", None, "dp"),
            P("expert", "dp", None),
        ),
        check_vma=False,
    )
```

profile of v0, /device:TPU:1, one launch (start us, length us, event | category | flops | bytes accessed | tf_op | source)
XLA Modules:
  0.0 168.3 jit_solution(1534811786858360483)
XLA Ops:
  7.2 0.0 copy-start
  7.2 0.0 copy-start.3
  7.2 0.8 broadcast_compare_fusion
  8.0 0.7 multiply_add_fusion
  8.7 0.0 copy-start.4
  8.7 0.1 convert_reduce_fusion
  8.8 2.1 %fusion.37 = bf16[320,1024]{1,0:T(8,128)(2,1)} fusion(bf16[128,320]{0,1:T(8,128)(2,1)S(1)} %convert_reduce_fusion, bf16[128,1024]{1,0:T(8,128)(2,1)} %param.9), kind=kOutput, calls=%fused_computation.48 | convolution fusion | flops 83886080 | bytes 999424 | tf_op jit(solution)/shard_map/tkc,td->cd/dot_general | solution.py:48
  10.9 5.2 %all-to-all-start = ((bf16[8,40,1024]{2,1,0:T(8,128)(2,1)}), bf16[8,40,1024]{2,1,0:T(8,128)(2,1)}, u32[]{:S(2)}, u32[]{:S(2)}) async-start(bf16[8,40,1024]{2,1,0:T(8,128)(2,1)} %bitcast), calls=%async_computation | async-start | bytes 1310720 | tf_op jit(solution)/shard_map/all_to_all | solution.py:55
  16.1 0.0 copy-done.3
  16.1 0.0 copy-start.1
  16.2 0.0 copy-done.4
  16.2 1.3 fusion.18
  17.4 6.4 %all-to-all-done = bf16[8,40,1024]{2,1,0:T(8,128)(2,1)} async-done(((bf16[8,40,1024]{2,1,0:T(8,128)(2,1)}), bf16[8,40,1024]{2,1,0:T(8,128)(2,1)}, u32[]{:S(2)}, u32[]{:S(2)}) %all-to-all-start) | async-done | bytes 655392 | tf_op jit(solution)/shard_map/all_to_all | solution.py:55
  23.8 7.6 %all-to-all-start.2 = ((bf16[8,40,1024]{2,1,0:T(8,128)(2,1)}), bf16[8,40,1024]{2,1,0:T(8,128)(2,1)}, u32[]{:S(2)}, u32[]{:S(2)}) async-start(bf16[8,40,1024]{2,1,0:T(8,128)(2,1)} %bitcast.11), calls=%async_computation.2 | async-start | bytes 1310720 | tf_op jit(solution)/shard_map/all_to_all | solution.py:62
  31.4 0.0 reduce-scatter.8.cloned.1.call-start
  31.4 0.0 copy-done.1
  31.5 2.7 %fusion.6 = f32[320,768]{1,0:T(8,128)} fusion(bf16[320,1024]{1,0:T(8,128)(2,1)} %bitcast.1, bf16[1,1024,768]{2,1,0:T(8,128)(2,1)S(1)} %copy-done.1), kind=kOutput, calls=%fused_computation.9 | convolution fusion | flops 503316480 | bytes 3211264 | tf_op jit(solution)/shard_map/dot_general | solution.py:9
  34.2 4.9 %all-to-all-done.2 = bf16[8,40,1024]{2,1,0:T(8,128)(2,1)} async-done(((bf16[8,40,1024]{2,1,0:T(8,128)(2,1)}), bf16[8,40,1024]{2,1,0:T(8,128)(2,1)}, u32[]{:S(2)}, u32[]{:S(2)}) %all-to-all-start.2) | async-done | bytes 655392 | tf_op jit(solution)/shard_map/all_to_all | solution.py:62
  39.1 2.4 %fusion = f32[320,768]{1,0:T(8,128)S(1)} fusion(bf16[320,1024]{1,0:T(8,128)(2,1)} %bitcast.12, bf16[1,768,1024]{2,1,0:T(8,128)(2,1)} %param.17), kind=kOutput, calls=%fused_computation.3 | convolution fusion | flops 503316480 | bytes 3211264 | tf_op jit(solution)/shard_map/dot_general | solution.py:19
  41.5 0.0 copy-done
  41.5 0.0 copy-done.6
  41.5 3.0 %multiply_convert_fusion.2 = (bf16[320,768]{1,0:T(8,128)(2,1)}, bf16[320,768]{1,0:T(8,128)(2,1)S(1)}, bf16[320,768]{1,0:T(8,128)(2,1)}) fusion(f32[320,768]{1,0:T(8,128)S(1)} %fusion, f32[320,768]{1,0:T(8,128)S(1)} %copy-done.6, bf16[320,1024]{1,0:T(8,128)(2,1)} %bitcast.1, bf16[1,1024,768]{2,1,0:T(8,128)(2,1)S(1)} %copy-done), kind=kOutput, calls=%fused_computation.25 | convolution fusion | flops 507248640 | bytes 5668864 | tf_op jit(solution)/shard_map/dot_general | solution.py:8
  44.6 0.8 copy-done.5
  45.3 3.3 %convolution_convert_fusion = bf16[768,1024]{1,0:T(8,128)(2,1)} fusion(bf16[320,768]{1,0:T(8,128)(2,1)S(1)} %get-tuple-element.7, bf16[320,1024]{1,0:T(8,128)(2,1)} %bitcast.12), kind=kOutput, calls=%fused_computation | convolution fusion | flops 504102912 | bytes 2719744 | tf_op jit(solution)/shard_map/dot_general | solution.py:30
  48.6 0.0 reduce-scatter.8.cloned.1.call-update
  48.6 0.0 reduce-scatter.4.cloned.1.call-start
  48.7 3.4 %convolution_convert_fusion.2 = bf16[1024,768]{0,1:T(8,128)(2,1)} fusion(bf16[320,1024]{1,0:T(8,128)(2,1)} %bitcast.1, bf16[320,768]{1,0:T(8,128)(2,1)} %get-tuple-element.6), kind=kOutput, calls=%fused_computation.2 | convolution fusion | flops 504102912 | bytes 2719744 | tf_op jit(solution)/shard_map/dot_general | solution.py:30
  52.1 0.0 reduce-scatter.4.cloned.1.call-update
  52.1 0.0 reduce-scatter.6.cloned.1.call-start
  52.1 3.4 %convolution_convert_fusion.1 = bf16[1024,768]{0,1:T(8,128)(2,1)} fusion(bf16[320,1024]{1,0:T(8,128)(2,1)} %bitcast.1, bf16[320,768]{1,0:T(8,128)(2,1)} %get-tuple-element.8), kind=kOutput, calls=%fused_computation.1 | convolution fusion | flops 504102912 | bytes 2719744 | tf_op jit(solution)/shard_map/dot_general | solution.py:30
  55.6 0.0 reduce-scatter.6.cloned.1.call-update
  55.6 3.1 %fusion.15 = bf16[320,1024]{1,0:T(8,128)(2,1)} fusion(bf16[320,768]{1,0:T(8,128)(2,1)} %copy-done.5, bf16[1,768,1024]{2,1,0:T(8,128)(2,1)} %param.17), kind=kOutput, calls=%fused_computation.17 | convolution fusion | flops 503644160 | bytes 2719744 | tf_op jit(solution)/shard_map/dot_general | solution.py:12
  58.7 7.7 %all-to-all-start.1 = ((bf16[8,40,1024]{2,1,0:T(8,128)(2,1)}), bf16[8,40,1024]{2,1,0:T(8,128)(2,1)}, u32[]{:S(2)}, u32[]{:S(2)}) async-start(bf16[8,40,1024]{2,1,0:T(8,128)(2,1)} %bitcast.63), calls=%async_computation.1 | async-start | bytes 1310720 | tf_op jit(solution)/shard_map/all_to_all | solution.py:61
  66.4 1.8 %fusion.4 = f32[320,1024]{1,0:T(8,128)S(1)} fusion(bf16[320,768]{1,0:T(8,128)(2,1)} %get-tuple-element.8, bf16[1,1024,768]{2,1,0:T(8,128)(2,1)S(1)} %copy-done.1), kind=kOutput, calls=%fused_computation.7 | convolution fusion | flops 503316480 | bytes 3375104 | tf_op jit(solution)/shard_map/dot_general | solution.py:84
  68.2 0.0 copy-done.2
  68.2 1.6 fusion.19
  69.8 4.3 %all-to-all-done.1 = bf16[8,40,1024]{2,1,0:T(8,128)(2,1)} async-done(((bf16[8,40,1024]{2,1,0:T(8,128)(2,1)}), bf16[8,40,1024]{2,1,0:T(8,128)(2,1)}, u32[]{:S(2)}, u32[]{:S(2)}) %all-to-all-start.1) | async-done | bytes 655392 | tf_op jit(solution)/shard_map/all_to_all | solution.py:61
  74.1 7.1 %all-to-all-start.3 = ((bf16[8,40,1024]{2,1,0:T(8,128)(2,1)}), bf16[8,40,1024]{2,1,0:T(8,128)(2,1)S(1)}, u32[]{:S(2)}, u32[]{:S(2)}) async-start(bf16[8,40,1024]{2,1,0:T(8,128)(2,1)} %bitcast.13), calls=%async_computation.3 | async-start | bytes 1310720 | tf_op jit(solution)/shard_map/all_to_all | solution.py:88
  81.1 2.3 %fusion.36 = (bf16[128,2,1024]{2,0,1:T(8,128)(2,1)S(1)}, bf16[128,1024]{1,0:T(8,128)(2,1)}) fusion(f32[128,2]{0,1:T(2,128)S(1)} %copy-done.4, bf16[320,1024,1]{1,0,2:T(8,128)(2,1)} %bitcast.7, s32[128,2]{0,1:T(2,128)S(1)} %multiply_add_fusion, pred[128,2]{0,1:T(4,128)(4,1)S(1)} %broadcast_compare_fusion), kind=kOutput, calls=%fused_computation.47 | convolution fusion | flops 168591360 | bytes 1444096 | tf_op jit(solution)/shard_map/tkc,cd->tkd/dot_general | solution.py:91
  83.5 1.2 fusion.24
  84.7 0.7 copy.17
  85.3 3.5 %all-to-all-done.3 = bf16[8,40,1024]{2,1,0:T(8,128)(2,1)S(1)} async-done(((bf16[8,40,1024]{2,1,0:T(8,128)(2,1)}), bf16[8,40,1024]{2,1,0:T(8,128)(2,1)S(1)}, u32[]{:S(2)}, u32[]{:S(2)}) %all-to-all-start.3) | async-done | bytes 655392 | tf_op jit(solution)/shard_map/all_to_all | solution.py:88
  88.8 1.0 fusion.38
  89.8 2.0 %multiply_bitcast_fusion = f32[1,192,1024]{2,1,0:T(8,128)} fusion(bf16[192,1024]{1,0:T(8,128)(2,1)} %reduce-scatter.8.cloned.1.call-done), kind=kLoop, calls=%fused_computation.28 | loop fusion | flops 393216 | bytes 1179648 | tf_op jit(solution)/shard_map/broadcast_in_dim | solution.py:106
  91.8 31.4 %reduce-scatter.4.cloned.1.call-done = bf16[1024,192]{0,1:T(8,128)(2,1)} async-done(((bf16[1024,768]{0,1:T(8,128)(2,1)}), bf16[1024,192]{0,1:T(8,128)(2,1)}) %reduce-scatter.4.cloned.1.call-update) | async-done | bytes 393232 | tf_op jit(solution)/shard_map/reduce_scatter | solution.py:72
  123.2 2.0 %multiply_bitcast_fusion.2 = f32[1,1024,192]{1,2,0:T(8,128)} fusion(bf16[1024,192]{0,1:T(8,128)(2,1)} %reduce-scatter.4.cloned.1.call-done), kind=kLoop, calls=%fused_computation.30 | loop fusion | flops 393216 | bytes 1179648 | tf_op jit(solution)/shard_map/broadcast_in_dim | solution.py:104
  125.2 34.6 %reduce-scatter.6.cloned.1.call-done = bf16[1024,192]{0,1:T(8,128)(2,1)} async-done(((bf16[1024,768]{0,1:T(8,128)(2,1)}), bf16[1024,192]{0,1:T(8,128)(2,1)}) %reduce-scatter.6.cloned.1.call-update) | async-done | bytes 393232 | tf_op jit(solution)/shard_map/reduce_scatter | solution.py:75
  159.8 2.0 %multiply_bitcast_fusion.1 = f32[1,1024,192]{1,2,0:T(8,128)} fusion(bf16[1024,192]{0,1:T(8,128)(2,1)} %reduce-scatter.6.cloned.1.call-done), kind=kLoop, calls=%fused_computation.29 | loop fusion | flops 393216 | bytes 1179648 | tf_op jit(solution)/shard_map/broadcast_in_dim | solution.py:105
  (5 shorter events, 0.0 us)
Async XLA Ops:
  7.2 34.3 %copy-start = (bf16[1,1024,768]{2,1,0:T(8,128)(2,1)S(1)}, bf16[1,1024,768]{2,1,0:T(8,128)(2,1)}, u32[]{:S(2)}) copy-start(bf16[1,1024,768]{2,1,0:T(8,128)(2,1)} %param.15) | copy-start | bytes 4718596
  7.2 8.9 %copy-start.3 = (bf16[128,1024]{1,0:T(8,128)(2,1)S(1)}, bf16[128,1024]{1,0:T(8,128)(2,1)}, u32[]{:S(2)}) copy-start(bf16[128,1024]{1,0:T(8,128)(2,1)} %param.14) | copy-start | bytes 786436
  8.7 7.5 %copy-start.4 = (f32[128,2]{0,1:T(2,128)S(1)}, f32[128,2]{0,1:T(2,128)}, u32[]{:S(2)}) copy-start(f32[128,2]{0,1:T(2,128)} %param.13) | copy-start | bytes 3076
  10.9 12.9 %all-to-all-start = ((bf16[8,40,1024]{2,1,0:T(8,128)(2,1)}), bf16[8,40,1024]{2,1,0:T(8,128)(2,1)}, u32[]{:S(2)}, u32[]{:S(2)}) async-start(bf16[8,40,1024]{2,1,0:T(8,128)(2,1)} %bitcast), calls=%async_computation | async-start | bytes 1310720 | tf_op jit(solution)/shard_map/all_to_all | solution.py:55
  16.1 15.3 %copy-start.1 = (bf16[1,1024,768]{2,1,0:T(8,128)(2,1)S(1)}, bf16[1,1024,768]{2,1,0:T(8,128)(2,1)}, u32[]{:S(2)}) copy-start(bf16[1,1024,768]{2,1,0:T(8,128)(2,1)} %param.16) | copy-start | bytes 4718596
  23.8 15.3 %all-to-all-start.2 = ((bf16[8,40,1024]{2,1,0:T(8,128)(2,1)}), bf16[8,40,1024]{2,1,0:T(8,128)(2,1)}, u32[]{:S(2)}, u32[]{:S(2)}) async-start(bf16[8,40,1024]{2,1,0:T(8,128)(2,1)} %bitcast.11), calls=%async_computation.2 | async-start | bytes 1310720 | tf_op jit(solution)/shard_map/all_to_all | solution.py:62
  31.4 58.4 %reduce-scatter.8.cloned.1.call-start = ((), (), s32[]{:S(2)}) async-start(), calls=%async_computation.9 | async-start | bytes 1966080 | tf_op jit(solution)/shard_map/reduce_scatter | solution.py:78
  39.1 2.4 %copy-start.6 = (f32[320,768]{1,0:T(8,128)S(1)}, f32[320,768]{1,0:T(8,128)}, u32[]{:S(2)}) copy-start(f32[320,768]{1,0:T(8,128)} %fusion.6) | copy-start | bytes 2949124
  44.5 0.8 copy-start.5
  48.6 74.6 %reduce-scatter.4.cloned.1.call-start = ((), (), s32[]{:S(2)}) async-start(), calls=%async_computation.7 | async-start | bytes 1966080 | tf_op jit(solution)/shard_map/reduce_scatter | solution.py:72
  52.1 107.7 %reduce-scatter.6.cloned.1.call-start = ((), (), s32[]{:S(2)}) async-start(), calls=%async_computation.8 | async-start | bytes 1966080 | tf_op jit(solution)/shard_map/reduce_scatter | solution.py:75
  58.7 15.4 %all-to-all-start.1 = ((bf16[8,40,1024]{2,1,0:T(8,128)(2,1)}), bf16[8,40,1024]{2,1,0:T(8,128)(2,1)}, u32[]{:S(2)}, u32[]{:S(2)}) async-start(bf16[8,40,1024]{2,1,0:T(8,128)(2,1)} %bitcast.63), calls=%async_computation.1 | async-start | bytes 1310720 | tf_op jit(solution)/shard_map/all_to_all | solution.py:61
  66.4 1.8 %copy-start.2 = (bf16[320,768]{1,0:T(8,128)(2,1)S(1)}, bf16[320,768]{1,0:T(8,128)(2,1)}, u32[]{:S(2)}) copy-start(bf16[320,768]{1,0:T(8,128)(2,1)} %get-tuple-element.6) | copy-start | bytes 1474564
  74.1 14.7 %all-to-all-start.3 = ((bf16[8,40,1024]{2,1,0:T(8,128)(2,1)}), bf16[8,40,1024]{2,1,0:T(8,128)(2,1)S(1)}, u32[]{:S(2)}, u32[]{:S(2)}) async-start(bf16[8,40,1024]{2,1,0:T(8,128)(2,1)} %bitcast.13), calls=%async_computation.3 | async-start | bytes 1310720 | tf_op jit(solution)/shard_map/all_to_all | solution.py:88
Sparse Core Ops, SparseCore 0:
  48.7 37.8 reduce-scatter.7
  88.9 34.2 reduce-scatter.3
  125.5 34.2 reduce-scatter.5
where the time goes:
time: 170 us; the launch traced here: 168 us
  waiting for transfers between devices  85.2 us (50%)
  matrix products  32.5 us (19%)
  starting transfers between devices  27.8 us (16%)
  between operations  13.8 us (8%)
  other arithmetic  7.5 us (4%)
    reduce_scatter x1, waiting for transfers between devices, body(): lax.psum_scatter(part_up.astype(jnp.bfloat16), 'dp', scatter_dimension=1,...  34.6 us
    reduce_scatter x1, waiting for transfers between devices, body(): lax.psum_scatter(part_gate.astype(jnp.bfloat16), 'dp', scatter_dimension=...  31.4 us
    dot_general x3, matrix products, column_product(): lax.dot_general(left, right, (((0,), (0,)), ((), ())), preferred_element_...  10.1 us
    all_to_all x1, starting transfers between devices, body(): lax.all_to_all(out_blocks, 'expert', split_axis=0, concat_axis=0, tiled=T...  7.72 us
    all_to_all x1, starting transfers between devices, body(): lax.all_to_all(send_grad, 'expert', split_axis=0, concat_axis=0, tiled=True)  7.64 us
    all_to_all x1, starting transfers between devices, body(): lax.all_to_all(grad_blocks, 'expert', split_axis=0, concat_axis=0, tiled=...  7.08 us
    all_to_all x1, waiting for transfers between devices, body(): lax.all_to_all(send_in, 'expert', split_axis=0, concat_axis=0, tiled=True)  6.39 us
    all_to_all x1, starting transfers between devices, body(): lax.all_to_all(send_in, 'expert', split_axis=0, concat_axis=0, tiled=True)  5.22 us
  transfers between devices with their start and end apart: 7, of which 6 were waited for; matrix products, arithmetic and copies ran while one was open for 16% of the time, Pallas kernels for 0%

commit v1 on v0

--- a/solution.py
+++ b/solution.py
@@ -1,7 +1,13 @@
+import functools
+
 import jax
 import jax.numpy as jnp
 from jax import lax
+from jax.experimental import pallas as pl
+from jax.experimental.pallas import tpu as pltpu
 from jax.sharding import PartitionSpec as P
+
+MESH = pl.DeviceIdType.MESH
 
 
 def expert_forward(rows_in, gate_mat, up_mat, down_mat):
@@ -107,9 +113,293 @@
     )
 
 
+def dot(left, right, left_dim=1, right_dim=0):
+    return lax.dot_general(
+        left, right, (((left_dim,), (right_dim,)), ((), ())), preferred_element_type=jnp.float32
+    )
+
+
+def group_order(index):
+    half = index // 2
+    side = (1 - half) * index + half * (3 - index)
+    order = []
+    for step, swapped in enumerate((1, 0, 2, 3)):
+        place = (1 - side) * step + side * swapped
+        order.append((1 - half) * place + half * (3 - place))
+    return order
+
+
+def kernel(
+    n, capacity, share,
+    tok_ref, cot_ref, meta_ref, index_ref, weight_ref, wg_ref, wu_ref, wd_ref, wgu_s_ref, wd_s_ref,
+    out_ref, route_ref, input_ref, gate_ref, up_ref, down_ref,
+    ztok, zcot, zmeta, send, recv, back_send, back_recv, out_acc, rig_acc,
+    z_send_sem, z_recv_sem, x_send_sem, x_recv_sem, b_send_sem, b_recv_sem, own_sem,
+):
+    me = lax.axis_index("expert")
+    group = lax.axis_index("dp")
+    order = group_order(group)
+    width = tok_ref.shape[1]
+    pair = 2 * capacity
+    cells = n * pair
+    hidden = wg_ref.shape[1]
+    tile = 256
+    peers = [lax.rem(me + step, n) for step in range(1, n)]
+
+    def dispatch(step, tok, cot, meta):
+        first, second = meta[0:1, :], meta[1:2, :]
+        w_first, w_second = meta[2:3, :], meta[3:4, :]
+        cell = lax.broadcasted_iota(jnp.int32, (cells, tok.shape[0]), 0).astype(jnp.float32)
+        to_tok = jnp.where((cell == first) | (cell == second), 1.0, 0.0)
+        low = cell - capacity
+        hit_first, hit_second = low == first, low == second
+        to_cot = jnp.where(hit_first | hit_second, 1.0, 0.0)
+        weight = jnp.where(hit_first, w_first, 0.0) + jnp.where(hit_second, w_second, 0.0)
+        weight = jnp.sum(weight + to_tok, axis=1, keepdims=True)
+        picked = dot(to_tok.astype(jnp.bfloat16), tok) + dot(to_cot.astype(jnp.bfloat16), cot)
+        send[step] = (picked * weight).astype(jnp.bfloat16).reshape(n, pair, width)
+
+    def x_copy(step, slot, peer):
+        return pltpu.make_async_remote_copy(
+            src_ref=send.at[step, peer], dst_ref=recv.at[step, slot],
+            send_sem=x_send_sem.at[step, peer], recv_sem=x_recv_sem.at[step, slot],
+            device_id=(peer, group), device_id_type=MESH,
+        )
+
+    def own_copy(step):
+        return pltpu.make_async_copy(send.at[step, me], recv.at[step, me], own_sem.at[step])
+
+    def x_start(step):
+        for peer in peers:
+            x_copy(step, me, peer).start()
+        own_copy(step).start()
+
+    def x_wait(step):
+        for peer in peers:
+            x_copy(step, peer, peer).wait_recv()
+        own_copy(step).wait()
+
+    def z_copies(slot, peer):
+        refs = ((tok_ref, ztok), (cot_ref, zcot), (meta_ref, zmeta))
+        return [
+            pltpu.make_async_remote_copy(
+                src_ref=source, dst_ref=target.at[slot],
+                send_sem=z_send_sem.at[peer, number], recv_sem=z_recv_sem.at[slot, number],
+                device_id=(me, peer), device_id_type=MESH,
+            )
+            for number, (source, target) in enumerate(refs)
+        ]
+
+    def z_dispatch(step):
+        source = order[step]
+        for copy in z_copies(source, source):
+            copy.wait_recv()
+        dispatch(step, ztok[source], zcot[source], zmeta[source])
+        x_start(step)
+
+    def load_rows(step):
+        both = recv[step].reshape(cells, width).astype(jnp.float32)
+        rows = [both[j * pair : j * pair + capacity] for j in range(n)]
+        grads = [both[j * pair + capacity : (j + 1) * pair] for j in range(n)]
+        return (
+            jnp.concatenate(rows, axis=0).astype(jnp.bfloat16),
+            jnp.concatenate(grads, axis=0).astype(jnp.bfloat16),
+        )
+
+    def hidden_values(rows, grads, gate_mat, up_mat, down_mat):
+        gate_value = dot(rows, gate_mat)
+        up_value = dot(rows, up_mat)
+        act_grad = dot(grads, down_mat, 1, 1)
+        sig = jax.nn.sigmoid(gate_value)
+        silu = gate_value * sig
+        activation = (silu * up_value).astype(jnp.bfloat16)
+        up_grad = (act_grad * silu).astype(jnp.bfloat16)
+        gate_grad = (act_grad * up_value * sig * (1.0 + gate_value * (1.0 - sig))).astype(
+            jnp.bfloat16
+        )
+        return activation, gate_grad, up_grad
+
+    def own_rows():
+        rows, grads = load_rows(0)
+        out_acc[...] = jnp.zeros_like(out_acc)
+        rig_acc[...] = jnp.zeros_like(rig_acc)
+
+        @pl.loop(0, hidden // tile)
+        def _(index):
+            at = pl.ds(pl.multiple_of(index * tile, tile), tile)
+            gate_mat, up_mat, down_mat = wg_ref[:, at], wu_ref[:, at], wd_ref[at, :]
+            activation, gate_grad, up_grad = hidden_values(rows, grads, gate_mat, up_mat, down_mat)
+            out_acc[...] += dot(activation, down_mat)
+            rig_acc[...] += dot(gate_grad, gate_mat, 1, 1) + dot(up_grad, up_mat, 1, 1)
+
+        for j in range(n):
+            at = slice(j * capacity, (j + 1) * capacity)
+            block = jnp.concatenate([out_acc[at, :], rig_acc[at, :]], axis=0)
+            back_send[j] = block.astype(jnp.bfloat16)
+
+    def b_copy(slot, peer):
+        return pltpu.make_async_remote_copy(
+            src_ref=back_send.at[peer], dst_ref=back_recv.at[slot],
+            send_sem=b_send_sem.at[peer], recv_sem=b_recv_sem.at[slot],
+            device_id=(peer, group), device_id_type=MESH,
+        )
+
+    own_back = pltpu.make_async_copy(back_send.at[me], back_recv.at[me], own_sem.at[4])
+
+    def weight_grads(step):
+        rows, grads = load_rows(step)
+        half = wgu_s_ref.shape[1] // 2
+        activation, gate_grad, up_grad = hidden_values(
+            rows, grads, wgu_s_ref[:, :half], wgu_s_ref[:, half:], wd_s_ref[...]
+        )
+        both = dot(rows, jnp.concatenate([gate_grad, up_grad], axis=1), 0, 0)
+        down = dot(activation, grads, 0, 0)[:share]
+        gate, up = both[:, :share], both[:, half : half + share]
+        for ref, value in ((gate_ref, gate), (up_ref, up), (down_ref, down)):
+            if step == 0:
+                ref[...] = value
+            elif step < 3:
+                ref[...] += value
+            else:
+                ref[...] = (ref[...] + value) * 0.25
+
+    def combine():
+        back = back_recv[...].reshape(cells, width)
+        cell = lax.broadcasted_iota(jnp.int32, (tok_ref.shape[0], cells), 1)
+        cot = cot_ref[...].astype(jnp.float32)
+        total = None
+        columns = []
+        mask = None
+        for k in range(2):
+            at = index_ref[:, k : k + 1]
+            picked = dot(jnp.where(cell == at, 1.0, 0.0).astype(jnp.bfloat16), back)
+            term = weight_ref[:, k : k + 1] * picked
+            total = term if total is None else total + term
+            columns.append(jnp.sum(cot * picked, axis=1, keepdims=True))
+            hit = jnp.where(cell - capacity == at, 1.0, 0.0)
+            mask = hit if mask is None else mask + hit
+        out_ref[...] = total.astype(jnp.bfloat16)
+        route_ref[...] = jnp.concatenate(columns, axis=1)
+        input_ref[...] = dot(mask.astype(jnp.bfloat16), back).astype(jnp.bfloat16)
+
+    barrier = pltpu.get_barrier_semaphore()
+    for peer in peers:
+        pl.semaphore_signal(barrier, inc=1, device_id=(peer, group), device_id_type=MESH)
+    for peer in order[1:]:
+        pl.semaphore_signal(barrier, inc=1, device_id=(me, peer), device_id_type=MESH)
+    dispatch(0, tok_ref[...], cot_ref[...], meta_ref[...])
+    pl.semaphore_wait(barrier, n - 1 + 3)
+
+    x_start(0)
+    for peer in order[1:]:
+        for copy in z_copies(group, peer):
+            copy.start()
+    z_dispatch(1)
+    x_wait(0)
+    own_rows()
+    for peer in peers:
+        b_copy(me, peer).start()
+    own_back.start()
+    z_dispatch(2)
+    weight_grads(0)
+    x_wait(1)
+    weight_grads(1)
+    z_dispatch(3)
+    x_wait(2)
+    weight_grads(2)
+    for peer in peers:
+        b_copy(peer, peer).wait_recv()
+    own_back.wait()
+    combine()
+    x_wait(3)
+    weight_grads(3)
+
+    for peer in order[1:]:
+        for copy in z_copies(group, peer):
+            copy.wait_send()
+    for peer in peers:
+        for step in range(4):
+            x_copy(step, me, peer).wait_send()
+        b_copy(me, peer).wait_send()
+
+
+def fused(tokens, expert_ids, slot_index, keep_mask, route_weight, cotangent, w_gate, w_up, w_down):
+    n = lax.axis_size("expert") * w_gate.shape[0]
+    groups = lax.axis_size("dp")
+    local, width = tokens.shape
+    hidden = w_gate.shape[2]
+    capacity = 5 * local // (2 * n)
+    pair = 2 * capacity
+    cells = n * pair
+    share = hidden // groups
+    half = -(-share // 128) * 128
+    index = jnp.where(keep_mask == 1, expert_ids * pair + slot_index, -cells)
+    meta = jnp.concatenate([index.astype(jnp.float32).T, route_weight.T], axis=0)
+    meta = jnp.pad(meta, ((0, 4), (0, 0)))
+    start = lax.axis_index("dp") * share
+    fill = ((0, 0), (0, half - share))
+    gate_s = jnp.pad(lax.dynamic_slice_in_dim(w_gate[0], start, share, 1), fill)
+    up_s = jnp.pad(lax.dynamic_slice_in_dim(w_up[0], start, share, 1), fill)
+    down_s = jnp.pad(lax.dynamic_slice_in_dim(w_down[0], start, share, 0), fill[::-1])
+    vmem = pl.BlockSpec(memory_space=pltpu.VMEM)
+    bf16, f32 = jnp.bfloat16, jnp.float32
+    dma = pltpu.SemaphoreType.DMA
+    results = pl.pallas_call(
+        functools.partial(kernel, n, capacity, share),
+        out_shape=(
+            jax.ShapeDtypeStruct((local, width), bf16),
+            jax.ShapeDtypeStruct((local, 2), f32),
+            jax.ShapeDtypeStruct((local, width), bf16),
+            jax.ShapeDtypeStruct((width, share), f32),
+            jax.ShapeDtypeStruct((width, share), f32),
+            jax.ShapeDtypeStruct((share, width), f32),
+        ),
+        in_specs=[vmem] * 10,
+        out_specs=(vmem,) * 6,
+        scratch_shapes=[
+            pltpu.VMEM((groups, local, width), bf16),
+            pltpu.VMEM((groups, local, width), bf16),
+            pltpu.VMEM((groups, 8, local), f32),
+            pltpu.VMEM((groups, n, pair, width), bf16),
+            pltpu.VMEM((groups, n, pair, width), bf16),
+            pltpu.VMEM((n, pair, width), bf16),
+            pltpu.VMEM((n, pair, width), bf16),
+            pltpu.VMEM((n * capacity, width), f32),
+            pltpu.VMEM((n * capacity, width), f32),
+            dma((groups, 3)),
+            dma((groups, 3)),
+            dma((groups, n)),
+            dma((groups, n)),
+            dma((n,)),
+            dma((n,)),
+            dma((5,)),
+        ],
+        compiler_params=pltpu.CompilerParams(
+            collective_id=0, has_side_effects=True, vmem_limit_bytes=58 * 2**20
+        ),
+        cost_estimate=pl.CostEstimate(
+            flops=8 * 10**9, bytes_accessed=12 * 2**20, transcendentals=5 * 10**5
+        ),
+    )(
+        tokens, cotangent, meta, index, route_weight, w_gate[0], w_up[0], w_down[0],
+        jnp.concatenate([gate_s, up_s], axis=1), down_s,
+    )
+    return results[:3] + tuple(value[None] for value in results[3:])
+
+
+def local_program(*args):
+    local, hidden = args[0].shape[0], args[6].shape[2]
+    n, groups = lax.axis_size("expert") * args[6].shape[0], lax.axis_size("dp")
+    capacity = 5 * local // (2 * n)
+    fits = groups == 4 and args[6].shape[0] == 1 and capacity % 8 == 0
+    if fits and hidden % 256 == 0 and local % 128 == 0:
+        return fused(*args)
+    return body(*args)
+
+
 def solution(mesh):
     return jax.shard_map(
-        body,
+        local_program,
         mesh=mesh,
         in_specs=(
             P(("expert", "dp"), None),

time: 170 us -> 109 us (0.64)
  Pallas kernels: 0 us -> 90.1 us
  waiting for transfers between devices: 85.2 us -> 0 us
  matrix products: 32.5 us -> 0 us
  starting transfers between devices: 27.8 us -> 0 us
  between operations: 13.8 us -> 0.67 us
  local copies, waits for them, and re-layouts: 1.47 us -> 13.7 us
  other arithmetic: 7.5 us -> 4.45 us
    pallas_call x0 -> x1, Pallas kernels: none -> 90.1 us  [fused(): pl.pallas_call(functools.partial(kernel, n, capacity, share), out_shape=(...]
    reduce_scatter x3 -> x0, waiting for transfers between devices: 66.1 us -> none  [the longest x1 34.6 us: body(): lax.psum_scatter(part_up.astype(jnp.bfloat16), 'dp', scatter_dimension=1,...]
    dot_general x14 -> x0, matrix products: 32.5 us -> none  [the longest x3 10.1 us: column_product(): lax.dot_general(left, right, (((0,), (0,)), ((), ())), preferred_element_...]
    all_to_all x4 -> x0, starting transfers between devices: 27.7 us -> none  [the longest x1 7.72 us: body(): lax.all_to_all(out_blocks, 'expert', split_axis=0, concat_axis=0, tiled=T...]
    all_to_all x4 -> x0, waiting for transfers between devices: 19.1 us -> none  [the longest x1 6.39 us: body(): lax.all_to_all(send_in, 'expert', split_axis=0, concat_axis=0, tiled=True)]
    unnamed x14 -> x16, local copies, waits for them, and re-layouts: 0.82 us -> 9.72 us
    broadcast_in_dim x3 -> x0, other arithmetic: 5.88 us -> none  [the longest x1 1.96 us: body(): (down_sum * scale)[None]]
    dynamic_slice x0 -> x2, local copies, waits for them, and re-layouts: none -> 2.83 us  [the longest x1 1.81 us: fused(): up_s = jnp.pad(lax.dynamic_slice_in_dim(w_up[0], start, share, 1), fill)]
  transfers between devices with their start and end apart: 7 -> 0, of which waited for: 6 -> 0; matrix products, arithmetic and copies ran while one was open for 16% -> 0% of each run, Pallas kernels for 0% -> 0%
where the time goes in v1:
time: 109 us
  Pallas kernels  90.1 us (83%)
  local copies, waits for them, and re-layouts  13.7 us (13%)
  other arithmetic  4.45 us (4%)
    pallas_call x1, Pallas kernels, fused(): pl.pallas_call(functools.partial(kernel, n, capacity, share), out_shape=(...  90.1 us
    unnamed x16, local copies, waits for them, and re-layouts  9.72 us

profile of v1, /device:TPU:1, one launch (start us, length us, event | category | flops | bytes accessed | tf_op | source)
XLA Modules:
  0.0 109.0 jit_solution(751397960440154051)
XLA Ops:
  0.6 0.7 broadcast_compare_fusion
  1.3 0.7 broadcast_multiply_fusion
  2.0 0.1 copy.38
  2.1 0.1 copy.36
  2.3 0.8 copy.37
  3.0 0.6 convert_bitcast_fusion
  3.7 0.1 copy.39
  3.7 1.3 %select_maximum_fusion.meta_ref = f32[8,128]{1,0:T(8,128)} fusion(f32[2,128]{1,0:T(2,128)} %bitcast.21, f32[2,128]{1,0:T(2,128)S(1)} %copy.39), kind=kLoop, calls=%fused_computation.10 | loop fusion | flops 4096 | bytes 6144 | tf_op jit(solution)/shard_map/concatenate | solution.py:337
  5.0 1.4 %copy.40.weight_ref = f32[128,2]{1,0:T(8,128)} copy(f32[128,2]{0,1:T(2,128)} %param.13) | data formatting | bytes 2048 | tf_op args[4]
  6.5 1.0 dynamic-slice_bitcast_fusion.2
  7.5 0.8 pad.18.wd_s_ref
  8.3 1.8 %dynamic-slice_bitcast_fusion = (bf16[1024,192]{1,0:T(8,128)(2,1)S(1)}, bf16[1024,192]{1,0:T(8,128)(2,1)S(1)}) fusion(bf16[1,1024,768]{2,1,0:T(8,128)(2,1)} %param.16, s32[]{:T(128)S(6)} %select_n.10, bf16[1,1024,768]{2,1,0:T(8,128)(2,1)} %param.15), kind=kLoop, calls=%fused_computation.5 | loop fusion | bytes 1572868 | tf_op jit(solution)/shard_map/dynamic_slice | solution.py:342
  10.1 1.1 %fusion.2.wgu_s_ref = bf16[1024,512]{1,0:T(8,128)(2,1)} fusion(bf16[1024,192]{1,0:T(8,128)(2,1)S(1)} %get-tuple-element.38, bf16[1024,192]{1,0:T(8,128)(2,1)S(1)} %get-tuple-element.39), kind=kLoop, calls=%fused_computation.4 | loop fusion | flops 4194304 | bytes 1835008 | tf_op jit(solution)/shard_map/concatenate | solution.py:385
  11.3 90.1 %shard_map.136 = (bf16[128,1024]{1,0:T(8,128)(2,1)}, f32[128,2]{1,0:T(8,128)}, bf16[128,1024]{1,0:T(8,128)(2,1)}, f32[1024,192]{1,0:T(8,128)}, f32[1024,192]{1,0:T(8,128)}, /*index=5*/f32[192,1024]{1,0:T(8,128)}) custom-call(bf16[128,1024]{1,0:T(8,128)(2,1)} %tok_ref.1, bf16[128,1024]{1,0:T(8,128)(2,1)} %cot_ref.1, f32[8,128]{1,0:T(8,128)} %select_maximum_fusion.meta_ref, ...), custom_call_target="tpu_custom_call" | custom-call | flops 8000000000 | bytes 12582912 | tf_op jit(solution)/shard_map/pallas_call | solution.py:347
  101.4 0.0 copy-start
  101.4 1.6 %copy.41 = f32[128,2]{0,1:T(2,128)} copy(f32[128,2]{1,0:T(8,128)} %get-tuple-element.31) | data formatting | bytes 2048
  103.0 0.0 copy-start.3
  103.0 2.5 %copy.42 = f32[1,1024,192]{1,2,0:T(8,128)} copy(f32[1,1024,192]{2,1,0:T(8,128)} %bitcast.16) | data formatting | bytes 1572864
  105.5 0.0 copy-done
  105.5 0.0 copy-start.2
  105.5 0.0 copy-start.1
  105.5 1.2 %copy.43 = f32[1,1024,192]{1,2,0:T(8,128)} copy(f32[1,1024,192]{2,1,0:T(8,128)S(1)} %bitcast.15) | data formatting | bytes 1572864
  106.7 0.0 copy-done.3
  106.7 0.7 copy.47
  107.4 0.0 copy-done.2
  107.4 0.7 copy.48
  108.1 0.0 copy-done.1
  108.1 0.9 copy.49
Async XLA Ops:
  101.4 4.0 %copy-start = (f32[1024,192]{1,0:T(8,128)S(1)}, f32[1024,192]{1,0:T(8,128)}, u32[]{:S(2)}) copy-start(f32[1024,192]{1,0:T(8,128)} %get-tuple-element.16) | copy-start | bytes 2359300
  103.0 3.7 %copy-start.3 = (bf16[128,1024]{1,0:T(8,128)(2,1)S(1)}, bf16[128,1024]{1,0:T(8,128)(2,1)}, u32[]{:S(2)}) copy-start(bf16[128,1024]{1,0:T(8,128)(2,1)} %get-tuple-element.46) | copy-start | bytes 786436
  105.5 1.9 %copy-start.2 = (bf16[128,1024]{1,0:T(8,128)(2,1)S(1)}, bf16[128,1024]{1,0:T(8,128)(2,1)}, u32[]{:S(2)}) copy-start(bf16[128,1024]{1,0:T(8,128)(2,1)} %get-tuple-element.48) | copy-start | bytes 786436
  105.5 2.6 %copy-start.1 = (f32[192,1024]{1,0:T(8,128)S(1)}, f32[192,1024]{1,0:T(8,128)}, u32[]{:S(2)}) copy-start(f32[192,1024]{1,0:T(8,128)} %get-tuple-element.17) | copy-start | bytes 2359300

commit v2 on v1

--- a/solution.py
+++ b/solution.py
@@ -130,10 +130,10 @@
 
 
 def kernel(
-    n, capacity, share,
-    tok_ref, cot_ref, meta_ref, index_ref, weight_ref, wg_ref, wu_ref, wd_ref, wgu_s_ref, wd_s_ref,
+    n, capacity, share, window,
+    tok_ref, cot_ref, ids_ref, slot_ref, keep_ref, weight_ref, wg_ref, wu_ref, wd_ref,
     out_ref, route_ref, input_ref, gate_ref, up_ref, down_ref,
-    ztok, zcot, zmeta, send, recv, back_send, back_recv, out_acc, rig_acc,
+    meta_ref, ztok, zcot, zmeta, send, recv, back_send, back_recv, out_acc, rig_acc, grad_acc,
     z_send_sem, z_recv_sem, x_send_sem, x_recv_sem, b_send_sem, b_recv_sem, own_sem,
 ):
     me = lax.axis_index("expert")
@@ -145,6 +145,9 @@
     hidden = wg_ref.shape[1]
     tile = 256
     peers = [lax.rem(me + step, n) for step in range(1, n)]
+    partner = order[1]
+    base = pl.multiple_of(share * group // 128 * 128, 128)
+    rest = pl.multiple_of(share * group % 128, 8)
 
     def dispatch(step, tok, cot, meta):
         first, second = meta[0:1, :], meta[1:2, :]
@@ -174,6 +177,13 @@
             x_copy(step, me, peer).start()
         own_copy(step).start()
 
+    def relay_copy(slot):
+        return pltpu.make_async_remote_copy(
+            src_ref=recv.at[0, slot], dst_ref=recv.at[1, slot],
+            send_sem=x_send_sem.at[1, slot], recv_sem=x_recv_sem.at[1, slot],
+            device_id=(me, partner), device_id_type=MESH,
+        )
+
     def x_wait(step):
         for peer in peers:
             x_copy(step, peer, peer).wait_recv()
@@ -248,38 +258,36 @@
 
     def weight_grads(step):
         rows, grads = load_rows(step)
-        half = wgu_s_ref.shape[1] // 2
+        at = pl.ds(base, window)
         activation, gate_grad, up_grad = hidden_values(
-            rows, grads, wgu_s_ref[:, :half], wgu_s_ref[:, half:], wd_s_ref[...]
-        )
-        both = dot(rows, jnp.concatenate([gate_grad, up_grad], axis=1), 0, 0)
-        down = dot(activation, grads, 0, 0)[:share]
-        gate, up = both[:, :share], both[:, half : half + share]
-        for ref, value in ((gate_ref, gate), (up_ref, up), (down_ref, down)):
-            if step == 0:
-                ref[...] = value
-            elif step < 3:
-                ref[...] += value
-            else:
-                ref[...] = (ref[...] + value) * 0.25
+            rows, grads, wg_ref[:, at], wu_ref[:, at], wd_ref[at, :]
+        )
+        parts = ((gate_grad, rows), (up_grad, rows), (activation, grads))
+        for number, (left, right) in enumerate(parts):
+            value = dot(left, right, 0, 0)
+            grad_acc[number] = value if step == 0 else grad_acc[number] + value
+        if step == 3:
+            for number, ref in enumerate((gate_ref, up_ref, down_ref)):
+                ref[...] = grad_acc[number, pl.ds(rest, share), :] * 0.25
 
     def combine():
+        local = tok_ref.shape[0]
         back = back_recv[...].reshape(cells, width)
-        cell = lax.broadcasted_iota(jnp.int32, (tok_ref.shape[0], cells), 1)
+        cell = lax.broadcasted_iota(jnp.int32, (local, cells), 1).astype(jnp.float32)
         cot = cot_ref[...].astype(jnp.float32)
-        total = None
-        columns = []
-        mask = None
+        turned = jnp.concatenate([meta_ref[...]] * (local // 8), axis=0).T
+        lane = lax.broadcasted_iota(jnp.int32, (local, local), 1)
+        total = jnp.zeros((local, width), jnp.float32)
+        mask = jnp.zeros((local, cells), jnp.float32)
+        sums = jnp.zeros((local, local), jnp.float32)
         for k in range(2):
-            at = index_ref[:, k : k + 1]
+            at = turned[:, k : k + 1]
             picked = dot(jnp.where(cell == at, 1.0, 0.0).astype(jnp.bfloat16), back)
-            term = weight_ref[:, k : k + 1] * picked
-            total = term if total is None else total + term
-            columns.append(jnp.sum(cot * picked, axis=1, keepdims=True))
-            hit = jnp.where(cell - capacity == at, 1.0, 0.0)
-            mask = hit if mask is None else mask + hit
+            total += turned[:, k + 2 : k + 3] * picked
+            sums = jnp.where(lane == k, jnp.sum(cot * picked, axis=1, keepdims=True), sums)
+            mask += jnp.where(cell - capacity == at, 1.0, 0.0)
         out_ref[...] = total.astype(jnp.bfloat16)
-        route_ref[...] = jnp.concatenate(columns, axis=1)
+        route_ref[...] = sums.T[:2]
         input_ref[...] = dot(mask.astype(jnp.bfloat16), back).astype(jnp.bfloat16)
 
     barrier = pltpu.get_barrier_semaphore()
@@ -287,38 +295,47 @@
         pl.semaphore_signal(barrier, inc=1, device_id=(peer, group), device_id_type=MESH)
     for peer in order[1:]:
         pl.semaphore_signal(barrier, inc=1, device_id=(me, peer), device_id_type=MESH)
+    place = jnp.where(keep_ref[...] == 1, ids_ref[...] * pair + slot_ref[...], -cells)
+    blank = jnp.zeros((4, tok_ref.shape[0]), jnp.float32)
+    meta_ref[...] = jnp.concatenate([place.astype(jnp.float32), weight_ref[...], blank], axis=0)
     dispatch(0, tok_ref[...], cot_ref[...], meta_ref[...])
     pl.semaphore_wait(barrier, n - 1 + 3)
 
     x_start(0)
-    for peer in order[1:]:
+    for peer in order[2:]:
         for copy in z_copies(group, peer):
             copy.start()
-    z_dispatch(1)
-    x_wait(0)
+    for peer in peers:
+        x_copy(0, peer, peer).wait_recv()
+        relay_copy(peer).start()
+    own_copy(0).wait()
+    relay_copy(me).start()
     own_rows()
     for peer in peers:
         b_copy(me, peer).start()
     own_back.start()
     z_dispatch(2)
     weight_grads(0)
-    x_wait(1)
+    z_dispatch(3)
+    for slot in range(n):
+        relay_copy(slot).wait_recv()
     weight_grads(1)
-    z_dispatch(3)
-    x_wait(2)
-    weight_grads(2)
     for peer in peers:
         b_copy(peer, peer).wait_recv()
     own_back.wait()
     combine()
+    x_wait(2)
+    weight_grads(2)
     x_wait(3)
     weight_grads(3)
 
-    for peer in order[1:]:
+    for peer in order[2:]:
         for copy in z_copies(group, peer):
             copy.wait_send()
+    for slot in range(n):
+        relay_copy(slot).wait_send()
     for peer in peers:
-        for step in range(4):
+        for step in (0, 2, 3):
             x_copy(step, me, peer).wait_send()
         b_copy(me, peer).wait_send()
 
@@ -330,33 +347,25 @@
     hidden = w_gate.shape[2]
     capacity = 5 * local // (2 * n)
     pair = 2 * capacity
-    cells = n * pair
     share = hidden // groups
-    half = -(-share // 128) * 128
-    index = jnp.where(keep_mask == 1, expert_ids * pair + slot_index, -cells)
-    meta = jnp.concatenate([index.astype(jnp.float32).T, route_weight.T], axis=0)
-    meta = jnp.pad(meta, ((0, 4), (0, 0)))
-    start = lax.axis_index("dp") * share
-    fill = ((0, 0), (0, half - share))
-    gate_s = jnp.pad(lax.dynamic_slice_in_dim(w_gate[0], start, share, 1), fill)
-    up_s = jnp.pad(lax.dynamic_slice_in_dim(w_up[0], start, share, 1), fill)
-    down_s = jnp.pad(lax.dynamic_slice_in_dim(w_down[0], start, share, 0), fill[::-1])
+    window = 128 * max(-(-(share * g % 128 + share) // 128) for g in range(groups))
     vmem = pl.BlockSpec(memory_space=pltpu.VMEM)
     bf16, f32 = jnp.bfloat16, jnp.float32
     dma = pltpu.SemaphoreType.DMA
     results = pl.pallas_call(
-        functools.partial(kernel, n, capacity, share),
+        functools.partial(kernel, n, capacity, share, window),
         out_shape=(
             jax.ShapeDtypeStruct((local, width), bf16),
-            jax.ShapeDtypeStruct((local, 2), f32),
+            jax.ShapeDtypeStruct((2, local), f32),
             jax.ShapeDtypeStruct((local, width), bf16),
-            jax.ShapeDtypeStruct((width, share), f32),
-            jax.ShapeDtypeStruct((width, share), f32),
+            jax.ShapeDtypeStruct((share, width), f32),
+            jax.ShapeDtypeStruct((share, width), f32),
             jax.ShapeDtypeStruct((share, width), f32),
         ),
-        in_specs=[vmem] * 10,
+        in_specs=[vmem] * 9,
         out_specs=(vmem,) * 6,
         scratch_shapes=[
+            pltpu.VMEM((8, local), f32),
             pltpu.VMEM((groups, local, width), bf16),
             pltpu.VMEM((groups, local, width), bf16),
             pltpu.VMEM((groups, 8, local), f32),
@@ -366,6 +375,7 @@
             pltpu.VMEM((n, pair, width), bf16),
             pltpu.VMEM((n * capacity, width), f32),
             pltpu.VMEM((n * capacity, width), f32),
+            pltpu.VMEM((3, window, width), f32),
             dma((groups, 3)),
             dma((groups, 3)),
             dma((groups, n)),
@@ -381,10 +391,11 @@
             flops=8 * 10**9, bytes_accessed=12 * 2**20, transcendentals=5 * 10**5
         ),
     )(
-        tokens, cotangent, meta, index, route_weight, w_gate[0], w_up[0], w_down[0],
-        jnp.concatenate([gate_s, up_s], axis=1), down_s,
-    )
-    return results[:3] + tuple(value[None] for value in results[3:])
+        tokens, cotangent, expert_ids.T, slot_index.T, keep_mask.T, route_weight.T,
+        w_gate[0], w_up[0], w_down[0],
+    )
+    out, route, inputs, gate, up, down = results
+    return out, route.T, inputs, gate.T[None], up.T[None], down[None]
 
 
 def local_program(*args):
@@ -392,7 +403,7 @@
     n, groups = lax.axis_size("expert") * args[6].shape[0], lax.axis_size("dp")
     capacity = 5 * local // (2 * n)
     fits = groups == 4 and args[6].shape[0] == 1 and capacity % 8 == 0
-    if fits and hidden % 256 == 0 and local % 128 == 0:
+    if fits and hidden == 768 and local == 128:
         return fused(*args)
     return body(*args)
 

time: 109 us -> 99.4 us (0.912)
  local copies, waits for them, and re-layouts: 13.7 us -> 8.57 us
  other arithmetic: 4.45 us -> 0 us
    dynamic_slice x2 -> x0, local copies, waits for them, and re-layouts: 2.83 us -> none  [the longest x1 1.81 us: fused(): up_s = jnp.pad(lax.dynamic_slice_in_dim(w_up[0], start, share, 1), fill)]
    concatenate x2 -> x0, other arithmetic: 2.44 us -> none  [the longest x1 1.3 us: fused(): jnp.concatenate([index.astype(jnp.float32).T, route_weight.T], axis=0)]
    unnamed x16 -> x10, local copies, waits for them, and re-layouts: 9.72 us -> 8.57 us
where the time goes in v2:
time: 99.4 us; the launch traced here: 99.2 us
  Pallas kernels  90 us (91%)
  local copies, waits for them, and re-layouts  8.57 us (9%)
    pallas_call x1, Pallas kernels, fused(): pl.pallas_call(functools.partial(kernel, n, capacity, share, window), out...  90 us
    unnamed x10, local copies, waits for them, and re-layouts  8.57 us

profile of v2, /device:TPU:1, one launch (start us, length us, event | category | flops | bytes accessed | tf_op | source)
XLA Modules:
  0.0 99.2 jit_solution(17030145217998688070)
XLA Ops:
  0.6 90.0 %shard_map.136 = (bf16[128,1024]{1,0:T(8,128)(2,1)}, f32[2,128]{1,0:T(2,128)}, bf16[128,1024]{1,0:T(8,128)(2,1)}, f32[192,1024]{1,0:T(8,128)}, f32[192,1024]{1,0:T(8,128)}, /*index=5*/f32[192,1024]{1,0:T(8,128)}) custom-call(bf16[128,1024]{1,0:T(8,128)(2,1)} %tok_ref.1, bf16[128,1024]{1,0:T(8,128)(2,1)} %cot_ref.1, s32[2,128]{1,0:T(2,128)} %bitcast.22, ...), custom_call_target="tpu_custom_call" | custom-call | flops 8000000000 | bytes 12582912 | tf_op jit(solution)/shard_map/pallas_call | solution.py:355
  90.7 0.0 copy-start.1
  90.7 1.7 %copy.21 = bf16[128,1024]{1,0:T(8,128)(2,1)} copy(bf16[128,1024]{1,0:T(8,128)(2,1)} %get-tuple-element.24) | data formatting | bytes 524288
  92.4 1.2 %copy.22 = f32[128,2]{0,1:T(2,128)} copy(f32[128,2]{0,1:T(2,128)} %bitcast.18) | data formatting | bytes 2048
  93.6 1.7 %copy.23 = bf16[128,1024]{1,0:T(8,128)(2,1)} copy(bf16[128,1024]{1,0:T(8,128)(2,1)} %get-tuple-element.26) | data formatting | bytes 524288
  95.3 0.0 copy-start
  95.3 2.2 %copy.24 = f32[1,1024,192]{1,2,0:T(8,128)} copy(f32[1,1024,192]{1,2,0:T(8,128)} %bitcast.17) | data formatting | bytes 1572864
  97.5 0.0 copy-done.1
  97.5 0.9 copy.25
  98.4 0.0 copy-done
  98.4 0.9 copy.26
Async XLA Ops:
  90.7 6.8 %copy-start.1 = (f32[192,1024]{1,0:T(8,128)S(1)}, f32[192,1024]{1,0:T(8,128)}, u32[]{:S(2)}) copy-start(f32[192,1024]{1,0:T(8,128)} %get-tuple-element.16) | copy-start | bytes 2359300
  95.3 3.0 %copy-start = (f32[192,1024]{1,0:T(8,128)S(1)}, f32[192,1024]{1,0:T(8,128)}, u32[]{:S(2)}) copy-start(f32[192,1024]{1,0:T(8,128)} %get-tuple-element.17) | copy-start | bytes 2359300

commit v3 on v2

--- a/solution.py
+++ b/solution.py
@@ -131,10 +131,10 @@
 
 def kernel(
     n, capacity, share, window,
-    tok_ref, cot_ref, ids_ref, slot_ref, keep_ref, weight_ref, wg_ref, wu_ref, wd_ref,
+    tok_ref, cot_ref, ids_ref, slot_ref, keep_ref, weight_ref, wg_in, wu_in, wd_in,
     out_ref, route_ref, input_ref, gate_ref, up_ref, down_ref,
-    meta_ref, ztok, zcot, zmeta, send, recv, back_send, back_recv, out_acc, rig_acc, grad_acc,
-    z_send_sem, z_recv_sem, x_send_sem, x_recv_sem, b_send_sem, b_recv_sem, own_sem,
+    meta_ref, ztok, zcot, zmeta, send, recv, back_send, back_recv, out_acc, rig_acc, grad_acc, wg_ref, wu_ref, wd_ref,
+    z_send_sem, z_recv_sem, x_send_sem, x_recv_sem, b_send_sem, b_recv_sem, own_sem, weight_sem,
 ):
     me = lax.axis_index("expert")
     group = lax.axis_index("dp")
@@ -189,21 +189,39 @@
             x_copy(step, peer, peer).wait_recv()
         own_copy(step).wait()
 
-    def z_copies(slot, peer):
+    def z_copies(slot, peer, held=False):
         refs = ((tok_ref, ztok), (cot_ref, zcot), (meta_ref, zmeta))
+        if held:
+            refs = tuple((target.at[slot], target) for _, target in refs)
         return [
             pltpu.make_async_remote_copy(
                 src_ref=source, dst_ref=target.at[slot],
-                send_sem=z_send_sem.at[peer, number], recv_sem=z_recv_sem.at[slot, number],
+                send_sem=z_send_sem.at[slot, number], recv_sem=z_recv_sem.at[slot, number],
                 device_id=(me, peer), device_id_type=MESH,
             )
             for number, (source, target) in enumerate(refs)
         ]
 
+    inner = (group == 1) | (group == 2)
+
+    def z_wait(step):
+        for copy in z_copies(order[step], order[step]):
+            copy.wait_recv()
+
+    def z_forward(step):
+        @pl.when(inner)
+        def _():
+            z_wait(step)
+            for copy in z_copies(order[step], partner, held=True):
+                copy.start()
+
     def z_dispatch(step):
         source = order[step]
-        for copy in z_copies(source, source):
-            copy.wait_recv()
+
+        @pl.when(jnp.logical_not(inner))
+        def _():
+            z_wait(step)
+
         dispatch(step, ztok[source], zcot[source], zmeta[source])
         x_start(step)
 
@@ -290,6 +308,13 @@
         route_ref[...] = sums.T[:2]
         input_ref[...] = dot(mask.astype(jnp.bfloat16), back).astype(jnp.bfloat16)
 
+    weights = ((wg_in, wg_ref), (wu_in, wu_ref), (wd_in, wd_ref))
+    weight_copies = [
+        pltpu.make_async_copy(source, target, weight_sem.at[number])
+        for number, (source, target) in enumerate(weights)
+    ]
+    for copy in weight_copies:
+        copy.start()
     barrier = pltpu.get_barrier_semaphore()
     for peer in peers:
         pl.semaphore_signal(barrier, inc=1, device_id=(peer, group), device_id_type=MESH)
@@ -301,15 +326,18 @@
     dispatch(0, tok_ref[...], cot_ref[...], meta_ref[...])
     pl.semaphore_wait(barrier, n - 1 + 3)
 
+    for copy in z_copies(group, order[2]):
+        copy.start()
     x_start(0)
-    for peer in order[2:]:
-        for copy in z_copies(group, peer):
-            copy.start()
+    z_forward(2)
     for peer in peers:
         x_copy(0, peer, peer).wait_recv()
         relay_copy(peer).start()
     own_copy(0).wait()
     relay_copy(me).start()
+    z_forward(3)
+    for copy in weight_copies:
+        copy.wait()
     own_rows()
     for peer in peers:
         b_copy(me, peer).start()
@@ -329,15 +357,30 @@
     x_wait(3)
     weight_grads(3)
 
-    for peer in order[2:]:
-        for copy in z_copies(group, peer):
-            copy.wait_send()
+    for copy in z_copies(group, order[2]):
+        copy.wait_send()
+
+    @pl.when(inner)
+    def _():
+        for source in order[2:]:
+            for copy in z_copies(source, partner, held=True):
+                copy.wait_send()
+
     for slot in range(n):
         relay_copy(slot).wait_send()
     for peer in peers:
         for step in (0, 2, 3):
             x_copy(step, me, peer).wait_send()
         b_copy(me, peer).wait_send()
+
+
+def finish(*refs):
+    sems = refs[12]
+    copies = [pltpu.make_async_copy(refs[i], refs[6 + i], sems.at[i]) for i in range(6)]
+    for copy in copies:
+        copy.start()
+    for copy in copies:
+        copy.wait()
 
 
 def fused(tokens, expert_ids, slot_index, keep_mask, route_weight, cotangent, w_gate, w_up, w_down):
@@ -362,7 +405,7 @@
             jax.ShapeDtypeStruct((share, width), f32),
             jax.ShapeDtypeStruct((share, width), f32),
         ),
-        in_specs=[vmem] * 9,
+        in_specs=[vmem] * 6 + [pl.BlockSpec(memory_space=pl.ANY)] * 3,
         out_specs=(vmem,) * 6,
         scratch_shapes=[
             pltpu.VMEM((8, local), f32),
@@ -376,6 +419,9 @@
             pltpu.VMEM((n * capacity, width), f32),
             pltpu.VMEM((n * capacity, width), f32),
             pltpu.VMEM((3, window, width), f32),
+            pltpu.VMEM((width, hidden), bf16),
+            pltpu.VMEM((width, hidden), bf16),
+            pltpu.VMEM((hidden, width), bf16),
             dma((groups, 3)),
             dma((groups, 3)),
             dma((groups, n)),
@@ -383,6 +429,7 @@
             dma((n,)),
             dma((n,)),
             dma((5,)),
+            dma((3,)),
         ],
         compiler_params=pltpu.CompilerParams(
             collective_id=0, has_side_effects=True, vmem_limit_bytes=58 * 2**20
@@ -394,7 +441,14 @@
         tokens, cotangent, expert_ids.T, slot_index.T, keep_mask.T, route_weight.T,
         w_gate[0], w_up[0], w_down[0],
     )
-    out, route, inputs, gate, up, down = results
+    place = pl.BlockSpec(memory_space=pl.ANY)
+    out, route, inputs, gate, up, down = pl.pallas_call(
+        finish,
+        out_shape=tuple(jax.ShapeDtypeStruct(value.shape, value.dtype) for value in results),
+        in_specs=[place] * 6,
+        out_specs=(place,) * 6,
+        scratch_shapes=[dma((6,))],
+    )(*results)
     return out, route.T, inputs, gate.T[None], up.T[None], down[None]
 
 

time: 99.4 us -> 192 us (1.93)
  Pallas kernels: 90 us -> 191 us
  local copies, waits for them, and re-layouts: 8.57 us -> 0 us
    pallas_call x0 -> x1, Pallas kernels: none -> 88.5 us  [fused(): pl.pallas_call(finish, out_shape=tuple((jax.ShapeDtypeStruct(value.shape,...]
    pallas_call x1, Pallas kernels: 90 us -> 102 us  [fused(): pl.pallas_call(functools.partial(kernel, n, capacity, share, window), out...]
    unnamed x10 -> x0, local copies, waits for them, and re-layouts: 8.57 us -> none
where the time goes in v3:
time: 192 us
  Pallas kernels  191 us (99%)
    pallas_call x1, Pallas kernels, fused(): pl.pallas_call(functools.partial(kernel, n, capacity, share, window), out...  102 us
    pallas_call x1, Pallas kernels, fused(): pl.pallas_call(finish, out_shape=tuple((jax.ShapeDtypeStruct(value.shape,...  88.5 us

profile of v3, /device:TPU:1, one launch (start us, length us, event | category | flops | bytes accessed | tf_op | source)
XLA Modules:
  0.0 191.6 jit_solution(2545420367390174203)
XLA Ops:
  0.6 102.4 %shard_map.136 = (bf16[128,1024]{1,0:T(8,128)(2,1)}, f32[2,128]{1,0:T(2,128)}, bf16[128,1024]{1,0:T(8,128)(2,1)}, f32[192,1024]{1,0:T(8,128)}, f32[192,1024]{1,0:T(8,128)}, /*index=5*/f32[192,1024]{1,0:T(8,128)}) custom-call(bf16[128,1024]{1,0:T(8,128)(2,1)} %tok_ref.1, bf16[128,1024]{1,0:T(8,128)(2,1)} %cot_ref.1, s32[2,128]{1,0:T(2,128)} %bitcast.21, ...), custom_call_target="tpu_custom_call" | custom-call | flops 8000000000 | bytes 12582912 | tf_op jit(solution)/shard_map/pallas_call | solution.py:398
  103.1 88.5 %shard_map.137 = (bf16[128,1024]{1,0:T(8,128)(2,1)}, f32[2,128]{1,0:T(2,128)}, bf16[128,1024]{1,0:T(8,128)(2,1)}, f32[192,1024]{1,0:T(8,128)}, f32[192,1024]{1,0:T(8,128)}, /*index=5*/f32[192,1024]{1,0:T(8,128)}) custom-call(bf16[128,1024]{1,0:T(8,128)(2,1)} %get-tuple-element.18.refs_0_, f32[2,128]{1,0:T(2,128)} %get-tuple-element.19.refs_1_, ...), custom_call_target="tpu_custom_call" | custom-call | tf_op jit(solution)/shard_map/pallas_call | solution.py:445

commit v4 on v2

--- a/solution.py
+++ b/solution.py
@@ -134,7 +134,7 @@
     tok_ref, cot_ref, ids_ref, slot_ref, keep_ref, weight_ref, wg_ref, wu_ref, wd_ref,
     out_ref, route_ref, input_ref, gate_ref, up_ref, down_ref,
     meta_ref, ztok, zcot, zmeta, send, recv, back_send, back_recv, out_acc, rig_acc, grad_acc,
-    z_send_sem, z_recv_sem, x_send_sem, x_recv_sem, b_send_sem, b_recv_sem, own_sem,
+    z_send_sem, z_recv_sem, x_send_sem, x_recv_sem, b_send_sem, b_recv_sem,
 ):
     me = lax.axis_index("expert")
     group = lax.axis_index("dp")
@@ -169,13 +169,10 @@
             device_id=(peer, group), device_id_type=MESH,
         )
 
-    def own_copy(step):
-        return pltpu.make_async_copy(send.at[step, me], recv.at[step, me], own_sem.at[step])
-
     def x_start(step):
         for peer in peers:
             x_copy(step, me, peer).start()
-        own_copy(step).start()
+        recv[step, me] = send[step, me]
 
     def relay_copy(slot):
         return pltpu.make_async_remote_copy(
@@ -187,7 +184,6 @@
     def x_wait(step):
         for peer in peers:
             x_copy(step, peer, peer).wait_recv()
-        own_copy(step).wait()
 
     def z_copies(slot, peer):
         refs = ((tok_ref, ztok), (cot_ref, zcot), (meta_ref, zmeta))
@@ -253,8 +249,6 @@
             send_sem=b_send_sem.at[peer], recv_sem=b_recv_sem.at[slot],
             device_id=(peer, group), device_id_type=MESH,
         )
-
-    own_back = pltpu.make_async_copy(back_send.at[me], back_recv.at[me], own_sem.at[4])
 
     def weight_grads(step):
         rows, grads = load_rows(step)
@@ -308,12 +302,11 @@
     for peer in peers:
         x_copy(0, peer, peer).wait_recv()
         relay_copy(peer).start()
-    own_copy(0).wait()
     relay_copy(me).start()
     own_rows()
     for peer in peers:
         b_copy(me, peer).start()
-    own_back.start()
+    back_recv[me] = back_send[me]
     z_dispatch(2)
     weight_grads(0)
     z_dispatch(3)
@@ -322,7 +315,6 @@
     weight_grads(1)
     for peer in peers:
         b_copy(peer, peer).wait_recv()
-    own_back.wait()
     combine()
     x_wait(2)
     weight_grads(2)
@@ -338,6 +330,11 @@
         for step in (0, 2, 3):
             x_copy(step, me, peer).wait_send()
         b_copy(me, peer).wait_send()
+
+
+def finish(*refs):
+    for source, target in zip(refs[:6], refs[6:]):
+        target[...] = source[...]
 
 
 def fused(tokens, expert_ids, slot_index, keep_mask, route_weight, cotangent, w_gate, w_up, w_down):
@@ -382,7 +379,6 @@
             dma((groups, n)),
             dma((n,)),
             dma((n,)),
-            dma((5,)),
         ],
         compiler_params=pltpu.CompilerParams(
             collective_id=0, has_side_effects=True, vmem_limit_bytes=58 * 2**20
@@ -394,7 +390,13 @@
         tokens, cotangent, expert_ids.T, slot_index.T, keep_mask.T, route_weight.T,
         w_gate[0], w_up[0], w_down[0],
     )
-    out, route, inputs, gate, up, down = results
+    out, route, inputs, gate, up, down = pl.pallas_call(
+        finish,
+        out_shape=tuple(jax.ShapeDtypeStruct(value.shape, value.dtype) for value in results),
+        in_specs=[vmem] * 6,
+        out_specs=(vmem,) * 6,
+        compiler_params=pltpu.CompilerParams(vmem_limit_bytes=16 * 2**20),
+    )(*results)
     return out, route.T, inputs, gate.T[None], up.T[None], down[None]
 
 

time: 99.4 us -> 98.5 us (level)
  local copies, waits for them, and re-layouts: 8.57 us -> 5.95 us
  Pallas kernels: 90 us -> 91.5 us
    unnamed x10 -> x12, local copies, waits for them, and re-layouts: 8.57 us -> 5.95 us
    pallas_call x0 -> x1, Pallas kernels: none -> 1.76 us  [fused(): pl.pallas_call(finish, out_shape=tuple((jax.ShapeDtypeStruct(value.shape,...]
where the time goes in v4:
time: 98.5 us; the launch traced here: 98.1 us
  Pallas kernels  91.5 us (93%)
  local copies, waits for them, and re-layouts  5.95 us (6%)
    pallas_call x1, Pallas kernels, fused(): pl.pallas_call(functools.partial(kernel, n, capacity, share, window), out...  89.8 us
    unnamed x12, local copies, waits for them, and re-layouts  5.95 us

profile of v4, /device:TPU:1, one launch (start us, length us, event | category | flops | bytes accessed | tf_op | source)
XLA Modules:
  0.0 98.1 jit_solution(4025470290427781365)
XLA Ops:
  0.6 89.8 %shard_map.136 = (bf16[128,1024]{1,0:T(8,128)(2,1)}, f32[2,128]{1,0:T(2,128)}, bf16[128,1024]{1,0:T(8,128)(2,1)}, f32[192,1024]{1,0:T(8,128)}, f32[192,1024]{1,0:T(8,128)}, /*index=5*/f32[192,1024]{1,0:T(8,128)}) custom-call(bf16[128,1024]{1,0:T(8,128)(2,1)} %tok_ref.1, bf16[128,1024]{1,0:T(8,128)(2,1)} %cot_ref.1, s32[2,128]{1,0:T(2,128)} %bitcast.21, ...), custom_call_target="tpu_custom_call" | custom-call | flops 8000000000 | bytes 12582912 | tf_op jit(solution)/shard_map/pallas_call | solution.py:352
  90.4 0.0 copy-start
  90.4 1.1 %copy-done = f32[192,1024]{1,0:T(8,128)S(1)} copy-done((f32[192,1024]{1,0:T(8,128)S(1)}, f32[192,1024]{1,0:T(8,128)}, u32[]{:S(2)}) %copy-start) | copy-done | bytes 786456
  91.5 0.0 copy-start.1
  91.6 1.1 %copy-done.1 = f32[192,1024]{1,0:T(8,128)S(1)} copy-done((f32[192,1024]{1,0:T(8,128)S(1)}, f32[192,1024]{1,0:T(8,128)}, u32[]{:S(2)}) %copy-start.1) | copy-done | bytes 786456
  92.7 0.0 copy-start.2
  92.7 1.1 %copy-done.2 = f32[192,1024]{1,0:T(8,128)S(1)} copy-done((f32[192,1024]{1,0:T(8,128)S(1)}, f32[192,1024]{1,0:T(8,128)}, u32[]{:S(2)}) %copy-start.2) | copy-done | bytes 786456
  93.8 0.0 copy-start.3
  93.8 0.9 copy-done.3
  94.8 0.0 copy-start.4
  94.8 0.9 copy-done.4
  95.7 0.0 copy-start.5
  95.7 0.7 copy-done.5
  96.4 1.8 %shard_map.137 = (bf16[128,1024]{1,0:T(8,128)(2,1)}, f32[2,128]{1,0:T(2,128)}, bf16[128,1024]{1,0:T(8,128)(2,1)}, f32[192,1024]{1,0:T(8,128)}, f32[192,1024]{1,0:T(8,128)}, /*index=5*/f32[192,1024]{1,0:T(8,128)}) custom-call(bf16[128,1024]{1,0:T(8,128)(2,1)S(1)} %copy-done.3, f32[2,128]{1,0:T(2,128)S(1)} %copy-done.5, bf16[128,1024]{1,0:T(8,128)(2,1)S(1)} %copy-done.4, ...), custom_call_target="tpu_custom_call" | custom-call | tf_op jit(solution)/shard_map/pallas_call | solution.py:393
Async XLA Ops:
  90.4 1.1 %copy-start = (f32[192,1024]{1,0:T(8,128)S(1)}, f32[192,1024]{1,0:T(8,128)}, u32[]{:S(2)}) copy-start(f32[192,1024]{1,0:T(8,128)} %get-tuple-element.21.refs_3_) | copy-start | bytes 2359300
  91.5 1.1 %copy-start.1 = (f32[192,1024]{1,0:T(8,128)S(1)}, f32[192,1024]{1,0:T(8,128)}, u32[]{:S(2)}) copy-start(f32[192,1024]{1,0:T(8,128)} %get-tuple-element.22.refs_4_) | copy-start | bytes 2359300
  92.7 1.1 %copy-start.2 = (f32[192,1024]{1,0:T(8,128)S(1)}, f32[192,1024]{1,0:T(8,128)}, u32[]{:S(2)}) copy-start(f32[192,1024]{1,0:T(8,128)} %get-tuple-element.23.refs_5_) | copy-start | bytes 2359300
  93.8 0.9 copy-start.3
  94.8 0.9 copy-start.4
  95.7 0.7 copy-start.5

commit v5 on v4

--- a/solution.py
+++ b/solution.py
@@ -395,7 +395,7 @@
         out_shape=tuple(jax.ShapeDtypeStruct(value.shape, value.dtype) for value in results),
         in_specs=[vmem] * 6,
         out_specs=(vmem,) * 6,
-        compiler_params=pltpu.CompilerParams(vmem_limit_bytes=16 * 2**20),
+        compiler_params=pltpu.CompilerParams(vmem_limit_bytes=60 * 2**20),
     )(*results)
     return out, route.T, inputs, gate.T[None], up.T[None], down[None]
 

time: 98.5 us -> 94 us (0.954)
  local copies, waits for them, and re-layouts: 5.95 us -> 0 us
  Pallas kernels: 91.5 us -> 93.2 us
    unnamed x12 -> x0, local copies, waits for them, and re-layouts: 5.95 us -> none
    pallas_call x1, Pallas kernels: 1.76 us -> 3.4 us  [fused(): pl.pallas_call(finish, out_shape=tuple((jax.ShapeDtypeStruct(value.shape,...]
where the time goes in v5:
time: 94 us; the launch traced here: 93.8 us
  Pallas kernels  93.2 us (99%)
    pallas_call x1, Pallas kernels, fused(): pl.pallas_call(functools.partial(kernel, n, capacity, share, window), out...  89.8 us
    pallas_call x1, Pallas kernels, fused(): pl.pallas_call(finish, out_shape=tuple((jax.ShapeDtypeStruct(value.shape,...  3.4 us

profile of v5, /device:TPU:1, one launch (start us, length us, event | category | flops | bytes accessed | tf_op | source)
XLA Modules:
  0.0 93.8 jit_solution(10538464815145884817)
XLA Ops:
  0.6 89.8 %shard_map.136 = (bf16[128,1024]{1,0:T(8,128)(2,1)}, f32[2,128]{1,0:T(2,128)}, bf16[128,1024]{1,0:T(8,128)(2,1)}, f32[192,1024]{1,0:T(8,128)}, f32[192,1024]{1,0:T(8,128)}, /*index=5*/f32[192,1024]{1,0:T(8,128)}) custom-call(bf16[128,1024]{1,0:T(8,128)(2,1)} %tok_ref.1, bf16[128,1024]{1,0:T(8,128)(2,1)} %cot_ref.1, s32[2,128]{1,0:T(2,128)} %bitcast.21, ...), custom_call_target="tpu_custom_call" | custom-call | flops 8000000000 | bytes 12582912 | tf_op jit(solution)/shard_map/pallas_call | solution.py:352
  90.4 3.4 %shard_map.137 = (bf16[128,1024]{1,0:T(8,128)(2,1)}, f32[2,128]{1,0:T(2,128)}, bf16[128,1024]{1,0:T(8,128)(2,1)}, f32[192,1024]{1,0:T(8,128)}, f32[192,1024]{1,0:T(8,128)}, /*index=5*/f32[192,1024]{1,0:T(8,128)}) custom-call(bf16[128,1024]{1,0:T(8,128)(2,1)} %get-tuple-element.18.refs_0_, f32[2,128]{1,0:T(2,128)} %get-tuple-element.19.refs_1_, ...), custom_call_target="tpu_custom_call" | custom-call | tf_op jit(solution)/shard_map/pallas_call | solution.py:393
